TPU v7x, 32 devices: a whole 2x2x4 slice. The times are simulated.
32 devices in a mesh: dom: 8 (over y, x, core), band: 4 (over z).
Axes of the slice: x: 2, y: 2, z: 4, core: 2. Of those that a mesh axis runs over, the one named last changes fastest.
Arguments:
- states: bfloat16 [256, 98304], P('band', 'dom'), may hold values from -640 to 640
- cell_kinetic: bfloat16 [512, 512], replicated, may hold values from -0.3 to 0.3, as said below
- cell_scale: float32 [256], P('dom'), may hold values from 0.5 to 2
- cell_potential: float32 [256, 512], P('dom'), may hold values from -0.3 to 0.3
- connectivity: int32 [256, 512], P('dom'), may hold values from 0 to 12287, as said below
- shared_nodes: int32 [8, 2, 1024], P('dom'), may hold values from 0 to 12287, as said below
- cell_counts: int32 [8], P('dom'), may hold values from 4 to 32, as said below
Outputs:
- rotated: bfloat16 [256, 98304], P('band', 'dom')
Inputs may be any that keep to these rules, and one draw needn't show every extreme that they name: cell_kinetic is symmetric. `connectivity`: row c of a domain (local cell number c) names each of the 512 nodes c * 3 * 128 to c * 3 * 128 + 511, counted round modulo 12288, exactly once. `shared_nodes`: the two rows of a domain name 2048 distinct nodes; position p of domain d's row 1 and of domain d+1's row 0 are the same physical node. `cell_counts`: in every draw some domain has all 32 cells live.
All inputs are finite; a program needn't handle non-finite values.
Results may differ from a plain program's by a relative error of at most 0.008.
Values may be sent and summed in bfloat16 or wider, within the bound.
A program may use at most 128 MiB of HBM per device.

v0:
```python
import functools

import jax
import jax.numpy as jnp
from jax import lax
from jax.experimental import pallas as pl
from jax.experimental.pallas import tpu as pltpu
from jax.sharding import PartitionSpec as P

CHEB = 4
NS_ITERS = 5
GROUP = 4
VMEM_LIMIT = 56 * 1024 * 1024
MESH = pl.DeviceIdType.MESH


def params():
    return pltpu.CompilerParams(vmem_limit_bytes=VMEM_LIMIT)


def vmem():
    return pl.BlockSpec(memory_space=pltpu.VMEM)


def smem():
    return pl.BlockSpec(memory_space=pltpu.SMEM)


def operators_kernel(node_total, counts_ref, conn_ref, pot_ref, kinetic_ref, ops_ref, diag_ref, ext):
    group, width, _ = ops_ref.shape
    step = 3 * width // 4
    first = pl.program_id(0) * group

    @pl.when(pl.program_id(0) == 0)
    def _():
        ext[...] = jnp.zeros_like(ext)

    for j in range(group):
        cell = first + j
        slots = conn_ref[pl.ds(cell, 1), :] - cell * step
        slots = jnp.where(slots < 0, slots + node_total, slots)
        hit = lax.broadcasted_iota(jnp.int32, (width, width), 0) == slots
        perm = jnp.where(hit, 1.0, 0.0).astype(jnp.bfloat16)
        rows = jnp.dot(perm, kinetic_ref[...], preferred_element_type=jnp.float32)
        ops_ref[j] = lax.dot_general(
            rows.astype(jnp.bfloat16), perm, (((1,), (1,)), ((), ())),
            preferred_element_type=jnp.float32,
        ).astype(jnp.bfloat16)
        alive = jnp.where(cell < counts_ref[0], 1.0, 0.0)
        column = jnp.sum(jnp.where(hit, pot_ref[pl.ds(cell, 1), :] * alive, 0.0), axis=1, keepdims=True)
        span = pl.ds(pl.multiple_of(cell * step, 128), width)
        ext[span, :] = ext[span, :] + column

    @pl.when(pl.program_id(0) == pl.num_programs(0) - 1)
    def _():
        tail = width - step
        half, lanes = diag_ref.shape
        ext[:tail] = ext[:tail] + ext[node_total:]
        low = lax.broadcasted_iota(jnp.int32, (ROWS, lanes), 1) < lanes // 2
        for i in range(half // ROWS):
            diag_ref[i * ROWS : (i + 1) * ROWS] = jnp.where(
                low, ext[i * ROWS : (i + 1) * ROWS], ext[half + i * ROWS : half + (i + 1) * ROWS]
            )


def operators(connectivity, cell_kinetic, cell_potential, cell_counts, node_total, state_rows):
    cells, width = connectivity.shape
    tail = width // 4
    blocks = cells // 2 // GROUP
    return pl.pallas_call(
        functools.partial(operators_kernel, node_total),
        grid=(cells // GROUP,),
        in_specs=[
            smem(),
            pl.BlockSpec((cells, width), lambda g: (0, 0)),
            pl.BlockSpec((cells, width), lambda g: (0, 0)),
            pl.BlockSpec((width, width), lambda g: (0, 0)),
        ],
        out_specs=[
            pl.BlockSpec((GROUP, width, width), lambda g: (g % blocks, g // blocks, 0)),
            pl.BlockSpec((node_total // 2, 2 * state_rows), lambda g: (0, 0)),
        ],
        out_shape=[
            jax.ShapeDtypeStruct((cells // 2, 2 * width, width), jnp.bfloat16),
            jax.ShapeDtypeStruct((node_total // 2, 2 * state_rows), jnp.float32),
        ],
        scratch_shapes=[pltpu.VMEM((node_total + tail, 1), jnp.float32)],
        compiler_params=params(),
        name="window_operators",
    )(cell_counts, connectivity, cell_potential, cell_kinetic)


CHUNK = 64


ROWS = 768


def by_rows(total, visit):
    def step(i, carry):
        visit(pl.multiple_of(i * ROWS, ROWS))
        return carry

    lax.fori_loop(0, total // ROWS, step, 0)


def swap_halves(value):
    lanes = value.shape[1]
    return jnp.concatenate([value[:, lanes // 2 :], value[:, : lanes // 2]], axis=1)


def add_faces(sides_ref, faces_ref, own_ref, from_refs, halo, total):
    shared = faces_ref.shape[1]
    for side, packed in enumerate(from_refs):
        half, lanes = packed.shape
        base = side * shared
        rows = jnp.where(sides_ref[side] > 0, packed[...].astype(jnp.float32), 0.0)
        rows = rows + own_ref[side * half : (side + 1) * half]
        halo[base : base + half] = rows[:, : lanes // 2]
        halo[base + half : base + shared] = rows[:, lanes // 2 :]
    for side in range(2):

        def visit(i, carry, side=side):
            base = i * CHUNK
            block = halo.at[pl.ds(pl.multiple_of(side * shared + base, CHUNK), CHUNK)]
            for j in range(CHUNK):
                total[pl.ds(faces_ref[side, base + j], 1), :] = block[j : j + 1, :]
            return carry

        lax.fori_loop(0, shared // CHUNK, visit, 0)


def pick_faces(faces_ref, total, halo, own_ref, to_refs):
    shared = faces_ref.shape[1]
    half = shared // 2
    for side in range(2):

        def visit(i, carry, side=side):
            base = i * CHUNK
            block = halo.at[pl.ds(pl.multiple_of(side * shared + base, CHUNK), CHUNK)]
            for j in range(CHUNK):
                block[j : j + 1, :] = total[pl.ds(faces_ref[side, base + j], 1), :]
            return carry

        lax.fori_loop(0, shared // CHUNK, visit, 0)
        base = side * shared
        rows = jnp.concatenate([halo[base : base + half], halo[base + half : base + shared]], axis=1)
        own_ref[side * half : (side + 1) * half] = rows
        to_refs[side][...] = rows.astype(to_refs[side].dtype)


def apply_cells(counts_ref, scale_ref, ops_ref, field, ext):
    group, _, width = ops_ref.shape
    step = 3 * width // 4
    lanes = ext.shape[1]
    low = lax.broadcasted_iota(jnp.int32, (1, lanes), 1) < lanes // 2
    for j in range(group):
        cell = pl.program_id(0) * group + j
        upper = cell + pl.num_programs(0) * group
        span = pl.ds(pl.multiple_of(cell * step, 128), width)
        scale = jnp.where(cell < counts_ref[0], scale_ref[cell], 0.0)
        upper_scale = jnp.where(upper < counts_ref[0], scale_ref[upper], 0.0)
        window = field[span, :]
        both = jnp.dot(ops_ref[j], window, preferred_element_type=jnp.float32)
        ext[span, :] = ext[span, :] + jnp.where(
            low, both[:width] * scale, both[width:] * upper_scale
        )


def finish_cells(faces_ref, local_ref, left_ref, right_ref, own_ref, ext, total, halo):
    half, lanes = local_ref.shape
    tail = ext.shape[0] - half
    ext[:tail] = ext[:tail] + swap_halves(ext[half:])

    def emit(base):
        value = ext[pl.ds(base, ROWS), :]
        local_ref[pl.ds(base, ROWS), :] = value
        total[pl.ds(base, ROWS), :] = value[:, : lanes // 2]
        total[pl.ds(half + base, ROWS), :] = value[:, lanes // 2 :]

    by_rows(half, emit)
    pick_faces(faces_ref, total, halo, own_ref, (left_ref, right_ref))


def start_tail(field, ext, half):
    tail = ext.shape[0] - half
    field[half:] = swap_halves(field[:tail])
    ext[half:] = jnp.zeros((tail, ext.shape[1]), jnp.float32)


def first_kernel(counts_ref, scale_ref, faces_ref, ops_ref, diag_ref, states_ref,
                 local_ref, left_ref, right_ref, own_ref, field_ref, field, ext, total, halo):
    half = local_ref.shape[0]

    @pl.when(pl.program_id(0) == 0)
    def _():
        def load(i, carry):
            low = pl.ds(pl.multiple_of(i * 128, 128), 128)
            high = pl.ds(pl.multiple_of(half + i * 128, 128), 128)
            pair = jnp.concatenate([states_ref[:, low], states_ref[:, high]], axis=0)
            value = pair.astype(jnp.float32).T
            rounded = value.astype(jnp.bfloat16)
            field[low, :] = rounded
            field_ref[low, :] = rounded
            ext[low, :] = value * diag_ref[low, :]
            return carry

        lax.fori_loop(0, half // 128, load, 0, unroll=6)
        start_tail(field, ext, half)

    apply_cells(counts_ref, scale_ref, ops_ref, field, ext)

    @pl.when(pl.program_id(0) == pl.num_programs(0) - 1)
    def _():
        finish_cells(faces_ref, local_ref, left_ref, right_ref, own_ref, ext, total, halo)


def unpack_local(old_ref, total):
    half, lanes = old_ref.shape

    def load(base):
        value = old_ref[pl.ds(base, ROWS), :]
        total[pl.ds(base, ROWS), :] = value[:, : lanes // 2]
        total[pl.ds(half + base, ROWS), :] = value[:, lanes // 2 :]

    by_rows(half, load)


def next_kernel(twice, counts_ref, scale_ref, faces_ref, sides_ref, ops_ref,
                diag_ref, prev_ref, old_ref, old_own, from_left, from_right,
                local_ref, left_ref, right_ref, own_ref, field_ref, field, ext, total, halo):
    half = local_ref.shape[0]

    @pl.when(pl.program_id(0) == 0)
    def _():
        unpack_local(old_ref, total)
        add_faces(sides_ref, faces_ref, old_own, (from_left, from_right), halo, total)

        def combine(base):
            rows = pl.ds(base, ROWS)
            value = jnp.concatenate([total[rows, :], total[pl.ds(half + base, ROWS), :]], axis=1)
            if twice:
                value = 2.0 * value - prev_ref[rows, :].astype(jnp.float32)
            value = value.astype(jnp.bfloat16)
            field[rows, :] = value
            field_ref[rows, :] = value
            ext[rows, :] = value.astype(jnp.float32) * diag_ref[rows, :]

        by_rows(half, combine)
        start_tail(field, ext, half)

    apply_cells(counts_ref, scale_ref, ops_ref, field, ext)

    @pl.when(pl.program_id(0) == pl.num_programs(0) - 1)
    def _():
        finish_cells(faces_ref, local_ref, left_ref, right_ref, own_ref, ext, total, halo)


def last_kernel(faces_ref, sides_ref, prev_ref, old_ref, old_own, from_left, from_right, field_ref,
                total, halo):
    half, lanes = old_ref.shape
    unpack_local(old_ref, total)
    add_faces(sides_ref, faces_ref, old_own, (from_left, from_right), halo, total)

    def combine(i, carry):
        low = pl.ds(pl.multiple_of(i * 128, 128), 128)
        high = pl.ds(pl.multiple_of(half + i * 128, 128), 128)
        value = jnp.concatenate([total[low, :], total[high, :]], axis=1)
        value = (2.0 * value - prev_ref[low, :].astype(jnp.float32)).T
        field_ref[:, low] = value[: lanes // 2].astype(jnp.bfloat16)
        field_ref[:, high] = value[lanes // 2 :].astype(jnp.bfloat16)
        return carry

    lax.fori_loop(0, half // 128, combine, 0, unroll=6)


def exchange_kernel(domains, left_ref, right_ref, from_left, from_right,
                    send_up, send_down, recv_up, recv_down):
    dom, band = lax.axis_index("dom"), lax.axis_index("band")
    barrier = pltpu.get_barrier_semaphore()
    has_left, has_right = dom > 0, dom < domains - 1

    @pl.when(has_left)
    def _():
        pl.semaphore_signal(barrier, inc=1, device_id=(dom - 1, band), device_id_type=MESH)

    @pl.when(has_right)
    def _():
        pl.semaphore_signal(barrier, inc=1, device_id=(dom + 1, band), device_id_type=MESH)

    pl.semaphore_wait(barrier, jnp.where(has_left & has_right, 2, 1))

    down = pltpu.make_async_remote_copy(
        src_ref=left_ref, dst_ref=from_right, send_sem=send_down, recv_sem=recv_down,
        device_id=(dom - 1, band), device_id_type=MESH)
    up = pltpu.make_async_remote_copy(
        src_ref=right_ref, dst_ref=from_left, send_sem=send_up, recv_sem=recv_up,
        device_id=(dom + 1, band), device_id_type=MESH)

    @pl.when(has_left)
    def _():
        down.start()

    @pl.when(has_right)
    def _():
        up.start()

    @pl.when(has_left)
    def _():
        down.wait_send()
        up.wait_recv()

    @pl.when(has_right)
    def _():
        up.wait_send()
        down.wait_recv()


def exchange(left, right):
    anywhere = pl.BlockSpec(memory_space=pl.ANY)
    return pl.pallas_call(
        functools.partial(exchange_kernel, lax.axis_size("dom")),
        in_specs=[anywhere] * 2,
        out_specs=[anywhere] * 2,
        out_shape=[jax.ShapeDtypeStruct(left.shape, left.dtype)] * 2,
        scratch_shapes=[pltpu.SemaphoreType.DMA] * 4,
        compiler_params=pltpu.CompilerParams(collective_id=1, has_side_effects=True),
        name="exchange",
    )(left, right)


def newton(gram_matrix):
    size = gram_matrix.shape[0]
    identity = (
        lax.broadcasted_iota(jnp.int32, (size, size), 0)
        == lax.broadcasted_iota(jnp.int32, (size, size), 1)
    ).astype(jnp.float32)
    frobenius = jnp.sqrt(jnp.sum(gram_matrix * gram_matrix))
    scaled = gram_matrix / frobenius
    inverse_root = None
    for repeat in range(NS_ITERS):
        if repeat == 0:
            factor = 1.5 * identity - 0.5 * scaled
            inverse_root = factor
        else:
            factor = 1.5 * identity - 0.5 * jnp.dot(
                inverse_root, scaled, precision=lax.Precision.HIGHEST
            )
            inverse_root = jnp.dot(factor, inverse_root, precision=lax.Precision.HIGHEST)
        if repeat < NS_ITERS - 1:
            scaled = jnp.dot(scaled, factor, precision=lax.Precision.HIGHEST)
    return inverse_root


def closing_kernel(domains, bands, filtered_ref, faces_ref, out_ref, shard, turned, mixing, part, weight,
                   from_dom, from_band, total,
                   send_in, recv_in, send_out, recv_out,
                   send_dom, recv_dom, send_band, recv_band, send_back, recv_back):
    dom, band = lax.axis_index("dom"), lax.axis_index("band")
    rows = part.shape[0] // domains
    state_rows = filtered_ref.shape[0]
    piece = shard.shape[1]

    def dom_peer(i):
        return (lax.rem(dom + i, domains), band)

    def band_peer(i):
        return (dom, lax.rem(band + i, bands))

    peers = [dom_peer(i) for i in range(1, domains)] + [band_peer(i) for i in range(1, bands)]
    barrier = pltpu.get_barrier_semaphore()
    for peer in peers:
        pl.semaphore_signal(barrier, inc=1, device_id=peer, device_id_type=MESH)
    pl.semaphore_wait(barrier, len(peers))

    def span(index):
        return pl.ds(pl.multiple_of(index * rows, 8), rows)

    def states_of(index):
        return pl.ds(pl.multiple_of(index * state_rows, state_rows), state_rows)

    def nodes_of(index):
        return pl.ds(pl.multiple_of(index * piece, 128), piece)

    regroup = []
    for i in range(1, bands):
        peer = band_peer(i)
        regroup.append(pltpu.make_async_remote_copy(
            src_ref=filtered_ref.at[:, nodes_of(peer[1])], dst_ref=shard.at[states_of(band)],
            send_sem=send_in.at[i], recv_sem=recv_in.at[i],
            device_id=peer, device_id_type=MESH))
    for copy in regroup:
        copy.start()
    shard[states_of(band), :] = filtered_ref[:, nodes_of(band)]
    part[...] = jnp.zeros_like(part)
    has_left = jnp.where(dom > 0, 1.0, 0.0)
    has_right = jnp.where(dom < domains - 1, 1.0, 0.0)

    def weigh(i, carry):
        shape = (128, faces_ref.shape[1])
        nodes = band * piece + i * 128 + lax.broadcasted_iota(jnp.int32, shape, 0)
        uses = jnp.where(faces_ref[0:1, :] == nodes, has_left, 0.0)
        uses = uses + jnp.where(faces_ref[1:2, :] == nodes, has_right, 0.0)
        column = 1.0 / (1.0 + jnp.sum(uses, axis=1, keepdims=True))
        row = jnp.broadcast_to(column, (128, 128)).T[:8]
        weight[:, pl.ds(pl.multiple_of(i * 128, 128), 128)] = row
        return carry

    lax.fori_loop(0, piece // 128, weigh, 0)
    for copy in regroup:
        copy.wait()

    def add_gram(i, carry):
        columns = pl.ds(pl.multiple_of(i * PIECE, PIECE), PIECE)
        value = shard[:, columns]
        part[...] += lax.dot_general(
            value * weight[0:1, columns].astype(jnp.bfloat16), value, (((1,), (1,)), ((), ())),
            preferred_element_type=jnp.float32)
        return carry

    lax.fori_loop(0, piece // PIECE, add_gram, 0)

    scatter = []
    for i in range(1, domains):
        peer = dom_peer(i)
        scatter.append(pltpu.make_async_remote_copy(
            src_ref=part.at[span(peer[0])], dst_ref=from_dom.at[i],
            send_sem=send_dom.at[i], recv_sem=recv_dom.at[i],
            device_id=peer, device_id_type=MESH))
    for copy in scatter:
        copy.start()
    own = part[span(dom), :]
    for copy in scatter:
        copy.wait()
    for i in range(1, domains):
        own = own + from_dom[i]
    from_band[band] = own
    across = []
    for i in range(1, bands):
        across.append(pltpu.make_async_remote_copy(
            src_ref=from_band.at[band], dst_ref=from_band.at[band],
            send_sem=send_band.at[i], recv_sem=recv_band.at[i],
            device_id=band_peer(i), device_id_type=MESH))
    for copy in across:
        copy.start()
    for copy in across:
        copy.wait()
    summed = from_band[0]
    for i in range(1, bands):
        summed = summed + from_band[i]
    total[span(dom), :] = summed
    back = []
    for i in range(1, domains):
        back.append(pltpu.make_async_remote_copy(
            src_ref=total.at[span(dom)], dst_ref=total.at[span(dom)],
            send_sem=send_back.at[i], recv_sem=recv_back.at[i],
            device_id=dom_peer(i), device_id_type=MESH))
    for copy in back:
        copy.start()
    for copy in back:
        copy.wait()
    mixing[...] = newton(total[...]).T.astype(jnp.bfloat16)

    def rotate(i, carry):
        columns = pl.ds(pl.multiple_of(i * PIECE, PIECE), PIECE)
        turned[:, columns] = jnp.dot(
            mixing[...], shard[:, columns], preferred_element_type=jnp.float32
        ).astype(jnp.bfloat16)
        return carry

    lax.fori_loop(0, piece // PIECE, rotate, 0)
    give = []
    for i in range(1, bands):
        peer = band_peer(i)
        give.append(pltpu.make_async_remote_copy(
            src_ref=turned.at[states_of(peer[1])], dst_ref=out_ref.at[:, nodes_of(band)],
            send_sem=send_out.at[i], recv_sem=recv_out.at[i],
            device_id=peer, device_id_type=MESH))
    for copy in give:
        copy.start()
    out_ref[:, nodes_of(band)] = turned[states_of(band), :]
    for copy in give:
        copy.wait()


PIECE = 512


def closing(filtered, faces):
    domains, bands = lax.axis_size("dom"), lax.axis_size("band")
    state_rows, nodes = filtered.shape
    size = bands * state_rows
    piece = nodes // bands
    rows = size // domains
    return pl.pallas_call(
        functools.partial(closing_kernel, domains, bands),
        in_specs=[vmem()] * 2,
        out_specs=vmem(),
        out_shape=jax.ShapeDtypeStruct(filtered.shape, jnp.bfloat16),
        scratch_shapes=[
            pltpu.VMEM((size, piece), jnp.bfloat16),
            pltpu.VMEM((size, piece), jnp.bfloat16),
            pltpu.VMEM((size, size), jnp.bfloat16),
            pltpu.VMEM((size, size), jnp.float32),
            pltpu.VMEM((8, piece), jnp.float32),
            pltpu.VMEM((domains, rows, size), jnp.float32),
            pltpu.VMEM((bands, rows, size), jnp.float32),
            pltpu.VMEM((size, size), jnp.float32),
        ] + [pltpu.SemaphoreType.DMA((bands,))] * 4
        + [pltpu.SemaphoreType.DMA((domains,))] * 2
        + [pltpu.SemaphoreType.DMA((bands,))] * 2
        + [pltpu.SemaphoreType.DMA((domains,))] * 2,
        compiler_params=pltpu.CompilerParams(
            vmem_limit_bytes=VMEM_LIMIT, collective_id=0, has_side_effects=True
        ),
        name="closing",
    )(filtered, faces)


def body(states, cell_kinetic, cell_scale, cell_potential, connectivity, shared_nodes, cell_counts):
    domain = lax.axis_index("dom")
    domains = lax.axis_size("dom")
    state_rows, node_total = states.shape
    cells, width = connectivity.shape
    faces = shared_nodes[0]
    shared = faces.shape[1]
    tail = width // 4
    half = node_total // 2
    lanes = 2 * state_rows
    ops, diag = operators(
        connectivity, cell_kinetic, cell_potential, cell_counts, node_total, state_rows
    )
    sides = jnp.stack([domain > 0, domain < domains - 1]).astype(jnp.int32)

    field_shape = jax.ShapeDtypeStruct((half, lanes), jnp.bfloat16)
    outs = [
        jax.ShapeDtypeStruct((half, lanes), jnp.float32),
        jax.ShapeDtypeStruct((shared // 2, lanes), jnp.bfloat16),
        jax.ShapeDtypeStruct((shared // 2, lanes), jnp.bfloat16),
        jax.ShapeDtypeStruct((shared, lanes), jnp.float32),
        field_shape,
    ]
    total_scratch = [
        pltpu.VMEM((node_total, state_rows), jnp.float32),
        pltpu.VMEM((2 * shared, state_rows), jnp.float32),
    ]
    scratch = [
        pltpu.VMEM((half + tail, lanes), jnp.bfloat16),
        pltpu.VMEM((half + tail, lanes), jnp.float32),
    ] + total_scratch
    group = GROUP // 2
    steps = cells // GROUP
    ops_spec = pl.BlockSpec((group, 2 * width, width), lambda g: (g, 0, 0))
    local, left, right, own, previous = pl.pallas_call(
        first_kernel,
        grid=(steps,),
        in_specs=[smem()] * 3 + [ops_spec] + [vmem()] * 2,
        out_specs=[vmem()] * 5,
        out_shape=outs,
        scratch_shapes=scratch,
        compiler_params=params(),
        name="apply_first",
    )(cell_counts, cell_scale, faces, ops, diag, states)
    current = previous
    for k in range(1, CHEB):
        halo = exchange(left, right)
        local, left, right, own, field = pl.pallas_call(
            functools.partial(next_kernel, k > 1),
            grid=(steps,),
            in_specs=[smem()] * 4 + [ops_spec] + [vmem()] * 6,
            out_specs=[vmem()] * 5,
            out_shape=outs,
            scratch_shapes=scratch,
            compiler_params=params(),
            name="apply_next",
        )(cell_counts, cell_scale, faces, sides, ops, diag, previous, local, own, *halo)
        previous = current
        current = field
    halo = exchange(left, right)
    filtered = pl.pallas_call(
        last_kernel,
        in_specs=[smem()] * 2 + [vmem()] * 5,
        out_specs=vmem(),
        out_shape=jax.ShapeDtypeStruct((state_rows, node_total), jnp.bfloat16),
        scratch_shapes=total_scratch,
        compiler_params=params(),
        name="finish",
    )(faces, sides, previous, local, own, *halo)
    return closing(filtered, faces)


def solution(mesh):
    in_specs = (
        P("band", "dom"),
        P(),
        P("dom"),
        P("dom", None),
        P("dom", None),
        P("dom", None, None),
        P("dom"),
    )
    out_specs = P("band", "dom")
    return jax.shard_map(body, mesh=mesh, in_specs=in_specs, out_specs=out_specs, check_vma=False)
```

profile of v0, /device:TPU:9, one launch (start us, length us, event | category | flops | bytes accessed | tf_op | source)
XLA Modules:
  0.0 271.6 jit_solution(14049955005498321309)
XLA Ops:
  0.7 0.6 add_convert_fusion.sides_ref
  1.3 25.6 %window_operators.1 = (bf16[16,1024,512]{2,1,0:T(8,128)(2,1)}, f32[6144,128]{1,0:T(8,128)}) custom-call(s32[1]{0:T(128)S(6)} %copy.9.counts_ref, s32[32,512]{1,0:T(8,128)} %conn_ref.1, f32[32,512]{1,0:T(8,128)} %pot_ref.1, bf16[512,512]{1,0:T(8,128)(2,1)} %kinetic_ref.1), custom_call_target="tpu_custom_call" | custom-call | tf_op jit(solution)/shard_map/window_operators/pallas_call | solution.py:70
  26.9 21.7 %apply_first.1 = (f32[6144,128]{1,0:T(8,128)}, bf16[512,128]{1,0:T(8,128)(2,1)}, bf16[512,128]{1,0:T(8,128)(2,1)}, f32[1024,128]{1,0:T(8,128)}, bf16[6144,128]{1,0:T(8,128)(2,1)}) custom-call(s32[1]{0:T(128)S(6)} %copy.9.counts_ref, f32[32]{0:T(128)} %scale_ref.7, s32[2,1024]{1,0:T(2,128)} %bitcast.3, bf16[16,1024,512]{2,1,0:T(8,128)(2,1)} %get-tuple-element.34.ops_ref, ...), custom_call_target="tpu_custom_call" | custom-call | tf_op jit(solution)/shard_map/apply_first/pallas_call | solution.py:554
  48.5 5.3 %exchange.4 = (bf16[512,128]{1,0:T(8,128)(2,1)}, bf16[512,128]{1,0:T(8,128)(2,1)}) custom-call(bf16[512,128]{1,0:T(8,128)(2,1)} %get-tuple-element.39.left_ref, bf16[512,128]{1,0:T(8,128)(2,1)} %get-tuple-element.40.right_ref), custom_call_target="tpu_custom_call" | custom-call | tf_op jit(solution)/shard_map/exchange/pallas_call | solution.py:321
  53.8 28.4 %apply_next.3 = (f32[6144,128]{1,0:T(8,128)}, bf16[512,128]{1,0:T(8,128)(2,1)}, bf16[512,128]{1,0:T(8,128)(2,1)}, f32[1024,128]{1,0:T(8,128)}, bf16[6144,128]{1,0:T(8,128)(2,1)}) custom-call(s32[1]{0:T(128)S(6)} %copy.9.counts_ref, f32[32]{0:T(128)} %scale_ref.7, s32[2,1024]{1,0:T(2,128)} %bitcast.4, s32[2]{0:T(128)} %add_convert_fusion.sides_ref, ...), custom_call_target="tpu_custom_call" | custom-call | tf_op jit(solution)/shard_map/apply_next/pallas_call | solution.py:567
  82.2 7.5 %exchange.5 = (bf16[512,128]{1,0:T(8,128)(2,1)}, bf16[512,128]{1,0:T(8,128)(2,1)}) custom-call(bf16[512,128]{1,0:T(8,128)(2,1)} %get-tuple-element.45.left_ref, bf16[512,128]{1,0:T(8,128)(2,1)} %get-tuple-element.46.right_ref), custom_call_target="tpu_custom_call" | custom-call | tf_op jit(solution)/shard_map/exchange/pallas_call | solution.py:321
  89.8 28.7 %apply_next.4 = (f32[6144,128]{1,0:T(8,128)}, bf16[512,128]{1,0:T(8,128)(2,1)}, bf16[512,128]{1,0:T(8,128)(2,1)}, f32[1024,128]{1,0:T(8,128)}, bf16[6144,128]{1,0:T(8,128)(2,1)}) custom-call(s32[1]{0:T(128)S(6)} %copy.9.counts_ref, f32[32]{0:T(128)} %scale_ref.7, s32[2,1024]{1,0:T(2,128)} %bitcast.5, s32[2]{0:T(128)} %add_convert_fusion.sides_ref, ...), custom_call_target="tpu_custom_call" | custom-call | tf_op jit(solution)/shard_map/apply_next/pallas_call | solution.py:567
  118.4 5.6 %exchange.6 = (bf16[512,128]{1,0:T(8,128)(2,1)}, bf16[512,128]{1,0:T(8,128)(2,1)}) custom-call(bf16[512,128]{1,0:T(8,128)(2,1)} %get-tuple-element.53.left_ref, bf16[512,128]{1,0:T(8,128)(2,1)} %get-tuple-element.54.right_ref), custom_call_target="tpu_custom_call" | custom-call | tf_op jit(solution)/shard_map/exchange/pallas_call | solution.py:321
  124.0 28.8 %apply_next.5 = (f32[6144,128]{1,0:T(8,128)}, bf16[512,128]{1,0:T(8,128)(2,1)}, bf16[512,128]{1,0:T(8,128)(2,1)}, f32[1024,128]{1,0:T(8,128)}, bf16[6144,128]{1,0:T(8,128)(2,1)}) custom-call(s32[1]{0:T(128)S(6)} %copy.9.counts_ref, f32[32]{0:T(128)} %scale_ref.7, s32[2,1024]{1,0:T(2,128)} %bitcast.6, s32[2]{0:T(128)} %add_convert_fusion.sides_ref, ...), custom_call_target="tpu_custom_call" | custom-call | tf_op jit(solution)/shard_map/apply_next/pallas_call | solution.py:567
  152.8 5.3 %exchange.7 = (bf16[512,128]{1,0:T(8,128)(2,1)}, bf16[512,128]{1,0:T(8,128)(2,1)}) custom-call(bf16[512,128]{1,0:T(8,128)(2,1)} %get-tuple-element.59.left_ref, bf16[512,128]{1,0:T(8,128)(2,1)} %get-tuple-element.60.right_ref), custom_call_target="tpu_custom_call" | custom-call | tf_op jit(solution)/shard_map/exchange/pallas_call | solution.py:321
  158.1 12.3 %finish.1.filtered_ref = bf16[64,12288]{1,0:T(8,128)(2,1)} custom-call(s32[2,1024]{1,0:T(2,128)} %bitcast.7, s32[2]{0:T(128)} %add_convert_fusion.sides_ref, bf16[6144,128]{1,0:T(8,128)(2,1)} %get-tuple-element.49.prev_ref, f32[6144,128]{1,0:T(8,128)} %get-tuple-element.57.old_ref, f32[1024,128]{1,0:T(8,128)} %get-tuple-element.58.old_own, ...), custom_call_target="tpu_custom_call" | custom-call | tf_op jit(solution)/shard_map/finish/pallas_call | solution.py:580
  170.4 98.6 %closing.1 = bf16[64,12288]{1,0:T(8,128)(2,1)} custom-call(bf16[64,12288]{1,0:T(8,128)(2,1)} %finish.1.filtered_ref, s32[2,1024]{1,0:T(2,128)} %bitcast.8), custom_call_target="tpu_custom_call" | custom-call | tf_op jit(solution)/shard_map/closing/pallas_call | solution.py:495
  269.0 2.7 copy.10
where the time goes:
time: 272 us
  Pallas kernels  268 us (99%)
    pallas_call x1, Pallas kernels, closing(): pl.pallas_call(functools.partial(closing_kernel, domains, bands), in_spec...  98.6 us
    pallas_call x3, Pallas kernels, body(): pl.pallas_call(functools.partial(next_kernel, k > 1), grid=(steps,), in_s...  85.8 us
    pallas_call x1, Pallas kernels, operators(): pl.pallas_call(functools.partial(operators_kernel, node_total), grid=(cel...  25.6 us
    pallas_call x4, Pallas kernels, exchange(): pl.pallas_call(functools.partial(exchange_kernel, lax.axis_size('dom')),...  23.6 us
    pallas_call x1, Pallas kernels, body(): pl.pallas_call(first_kernel, grid=(steps,), in_specs=[smem()] * 3 + [ops_...  21.7 us
    pallas_call x1, Pallas kernels, body(): pl.pallas_call(last_kernel, in_specs=[smem()] * 2 + [vmem()] * 5, out_spe...  12.3 us

commit v1 on v0

--- a/solution.py
+++ b/solution.py
@@ -10,12 +10,11 @@
 CHEB = 4
 NS_ITERS = 5
 GROUP = 4
-VMEM_LIMIT = 56 * 1024 * 1024
 MESH = pl.DeviceIdType.MESH
 
 
-def params():
-    return pltpu.CompilerParams(vmem_limit_bytes=VMEM_LIMIT)
+def params(mib=56):
+    return pltpu.CompilerParams(vmem_limit_bytes=mib * 1024 * 1024)
 
 
 def vmem():
@@ -26,15 +25,34 @@
     return pl.BlockSpec(memory_space=pltpu.SMEM)
 
 
-def operators_kernel(node_total, counts_ref, conn_ref, pot_ref, kinetic_ref, ops_ref, diag_ref, ext):
+def operators_kernel(counts_ref, scale_ref, faces_ref, conn_ref, pot_ref, kinetic_ref, states_ref,
+                     ops_ref, diag_ref, local_ref, left_ref, right_ref, own_ref, field_ref,
+                     column_sum, field, ext, total, halo):
     group, width, _ = ops_ref.shape
     step = 3 * width // 4
+    half, lanes = local_ref.shape
+    node_total = 2 * half
     first = pl.program_id(0) * group
+    pairs = pl.num_programs(0) * group // 2
 
     @pl.when(pl.program_id(0) == 0)
     def _():
-        ext[...] = jnp.zeros_like(ext)
-
+        column_sum[...] = jnp.zeros_like(column_sum)
+
+        def load(i, carry):
+            low = pl.ds(pl.multiple_of(i * 128, 128), 128)
+            high = pl.ds(pl.multiple_of(half + i * 128, 128), 128)
+            pair = jnp.concatenate([states_ref[:, low], states_ref[:, high]], axis=0)
+            rounded = pair.astype(jnp.float32).T.astype(jnp.bfloat16)
+            field[low, :] = rounded
+            field_ref[low, :] = rounded
+            ext[low, :] = jnp.zeros((128, lanes), jnp.float32)
+            return carry
+
+        lax.fori_loop(0, half // 128, load, 0, unroll=6)
+        start_tail(field, ext, half)
+
+    low_lane = lax.broadcasted_iota(jnp.int32, (1, lanes), 1) < lanes // 2
     for j in range(group):
         cell = first + j
         slots = conn_ref[pl.ds(cell, 1), :] - cell * step
@@ -42,52 +60,40 @@
         hit = lax.broadcasted_iota(jnp.int32, (width, width), 0) == slots
         perm = jnp.where(hit, 1.0, 0.0).astype(jnp.bfloat16)
         rows = jnp.dot(perm, kinetic_ref[...], preferred_element_type=jnp.float32)
-        ops_ref[j] = lax.dot_general(
+        operator = lax.dot_general(
             rows.astype(jnp.bfloat16), perm, (((1,), (1,)), ((), ())),
             preferred_element_type=jnp.float32,
         ).astype(jnp.bfloat16)
+        ops_ref[j] = operator
         alive = jnp.where(cell < counts_ref[0], 1.0, 0.0)
-        column = jnp.sum(jnp.where(hit, pot_ref[pl.ds(cell, 1), :] * alive, 0.0), axis=1, keepdims=True)
+        column = jnp.sum(
+            jnp.where(hit, pot_ref[pl.ds(cell, 1), :] * alive, 0.0), axis=1, keepdims=True
+        )
         span = pl.ds(pl.multiple_of(cell * step, 128), width)
-        ext[span, :] = ext[span, :] + column
+        column_sum[span, :] = column_sum[span, :] + column
+        upper = cell >= pairs
+        scale = alive * scale_ref[cell]
+        spread = jnp.where(
+            low_lane, jnp.where(upper, 0.0, scale), jnp.where(upper, scale, 0.0)
+        )
+        place = jnp.where(upper, cell - pairs, cell)
+        packed = pl.ds(pl.multiple_of(place * step, 128), width)
+        product = jnp.dot(operator, field[packed, :], preferred_element_type=jnp.float32)
+        ext[packed, :] = ext[packed, :] + product * spread
 
     @pl.when(pl.program_id(0) == pl.num_programs(0) - 1)
     def _():
         tail = width - step
-        half, lanes = diag_ref.shape
-        ext[:tail] = ext[:tail] + ext[node_total:]
-        low = lax.broadcasted_iota(jnp.int32, (ROWS, lanes), 1) < lanes // 2
-        for i in range(half // ROWS):
-            diag_ref[i * ROWS : (i + 1) * ROWS] = jnp.where(
-                low, ext[i * ROWS : (i + 1) * ROWS], ext[half + i * ROWS : half + (i + 1) * ROWS]
-            )
-
-
-def operators(connectivity, cell_kinetic, cell_potential, cell_counts, node_total, state_rows):
-    cells, width = connectivity.shape
-    tail = width // 4
-    blocks = cells // 2 // GROUP
-    return pl.pallas_call(
-        functools.partial(operators_kernel, node_total),
-        grid=(cells // GROUP,),
-        in_specs=[
-            smem(),
-            pl.BlockSpec((cells, width), lambda g: (0, 0)),
-            pl.BlockSpec((cells, width), lambda g: (0, 0)),
-            pl.BlockSpec((width, width), lambda g: (0, 0)),
-        ],
-        out_specs=[
-            pl.BlockSpec((GROUP, width, width), lambda g: (g % blocks, g // blocks, 0)),
-            pl.BlockSpec((node_total // 2, 2 * state_rows), lambda g: (0, 0)),
-        ],
-        out_shape=[
-            jax.ShapeDtypeStruct((cells // 2, 2 * width, width), jnp.bfloat16),
-            jax.ShapeDtypeStruct((node_total // 2, 2 * state_rows), jnp.float32),
-        ],
-        scratch_shapes=[pltpu.VMEM((node_total + tail, 1), jnp.float32)],
-        compiler_params=params(),
-        name="window_operators",
-    )(cell_counts, connectivity, cell_potential, cell_kinetic)
+        column_sum[:tail] = column_sum[:tail] + column_sum[node_total:]
+
+        def weigh(base):
+            rows = pl.ds(base, ROWS)
+            value = jnp.where(low_lane, column_sum[rows, :], column_sum[pl.ds(half + base, ROWS), :])
+            diag_ref[rows, :] = value
+            ext[rows, :] = ext[rows, :] + value * field[rows, :].astype(jnp.float32)
+
+        by_rows(half, weigh)
+        finish_cells(faces_ref, local_ref, left_ref, right_ref, own_ref, ext, total, halo)
 
 
 CHUNK = 64
@@ -188,33 +194,6 @@
     ext[half:] = jnp.zeros((tail, ext.shape[1]), jnp.float32)
 
 
-def first_kernel(counts_ref, scale_ref, faces_ref, ops_ref, diag_ref, states_ref,
-                 local_ref, left_ref, right_ref, own_ref, field_ref, field, ext, total, halo):
-    half = local_ref.shape[0]
-
-    @pl.when(pl.program_id(0) == 0)
-    def _():
-        def load(i, carry):
-            low = pl.ds(pl.multiple_of(i * 128, 128), 128)
-            high = pl.ds(pl.multiple_of(half + i * 128, 128), 128)
-            pair = jnp.concatenate([states_ref[:, low], states_ref[:, high]], axis=0)
-            value = pair.astype(jnp.float32).T
-            rounded = value.astype(jnp.bfloat16)
-            field[low, :] = rounded
-            field_ref[low, :] = rounded
-            ext[low, :] = value * diag_ref[low, :]
-            return carry
-
-        lax.fori_loop(0, half // 128, load, 0, unroll=6)
-        start_tail(field, ext, half)
-
-    apply_cells(counts_ref, scale_ref, ops_ref, field, ext)
-
-    @pl.when(pl.program_id(0) == pl.num_programs(0) - 1)
-    def _():
-        finish_cells(faces_ref, local_ref, left_ref, right_ref, own_ref, ext, total, halo)
-
-
 def unpack_local(old_ref, total):
     half, lanes = old_ref.shape
 
@@ -324,7 +303,9 @@
         out_specs=[anywhere] * 2,
         out_shape=[jax.ShapeDtypeStruct(left.shape, left.dtype)] * 2,
         scratch_shapes=[pltpu.SemaphoreType.DMA] * 4,
-        compiler_params=pltpu.CompilerParams(collective_id=1, has_side_effects=True),
+        compiler_params=pltpu.CompilerParams(
+            vmem_limit_bytes=4 * 1024 * 1024, collective_id=1, has_side_effects=True
+        ),
         name="exchange",
     )(left, right)
 
@@ -511,7 +492,7 @@
         + [pltpu.SemaphoreType.DMA((bands,))] * 2
         + [pltpu.SemaphoreType.DMA((domains,))] * 2,
         compiler_params=pltpu.CompilerParams(
-            vmem_limit_bytes=VMEM_LIMIT, collective_id=0, has_side_effects=True
+            vmem_limit_bytes=24 * 1024 * 1024, collective_id=0, has_side_effects=True
         ),
         name="closing",
     )(filtered, faces)
@@ -527,9 +508,6 @@
     tail = width // 4
     half = node_total // 2
     lanes = 2 * state_rows
-    ops, diag = operators(
-        connectivity, cell_kinetic, cell_potential, cell_counts, node_total, state_rows
-    )
     sides = jnp.stack([domain > 0, domain < domains - 1]).astype(jnp.int32)
 
     field_shape = jax.ShapeDtypeStruct((half, lanes), jnp.bfloat16)
@@ -551,16 +529,22 @@
     group = GROUP // 2
     steps = cells // GROUP
     ops_spec = pl.BlockSpec((group, 2 * width, width), lambda g: (g, 0, 0))
-    local, left, right, own, previous = pl.pallas_call(
-        first_kernel,
-        grid=(steps,),
-        in_specs=[smem()] * 3 + [ops_spec] + [vmem()] * 2,
-        out_specs=[vmem()] * 5,
-        out_shape=outs,
-        scratch_shapes=scratch,
+    blocks = cells // 2 // GROUP
+    ops, diag, local, left, right, own, previous = pl.pallas_call(
+        operators_kernel,
+        grid=(cells // GROUP,),
+        in_specs=[smem()] * 3 + [vmem()] * 4,
+        out_specs=[
+            pl.BlockSpec((GROUP, width, width), lambda g: (g % blocks, g // blocks, 0)),
+        ] + [vmem()] * 6,
+        out_shape=[
+            jax.ShapeDtypeStruct((cells // 2, 2 * width, width), jnp.bfloat16),
+            jax.ShapeDtypeStruct((half, lanes), jnp.float32),
+        ] + outs,
+        scratch_shapes=[pltpu.VMEM((node_total + tail, 1), jnp.float32)] + scratch,
         compiler_params=params(),
-        name="apply_first",
-    )(cell_counts, cell_scale, faces, ops, diag, states)
+        name="operators_and_first_apply",
+    )(cell_counts, cell_scale, faces, connectivity, cell_potential, cell_kinetic, states)
     current = previous
     for k in range(1, CHEB):
         halo = exchange(left, right)
@@ -571,7 +555,7 @@
             out_specs=[vmem()] * 5,
             out_shape=outs,
             scratch_shapes=scratch,
-            compiler_params=params(),
+            compiler_params=params(32),
             name="apply_next",
         )(cell_counts, cell_scale, faces, sides, ops, diag, previous, local, own, *halo)
         previous = current
@@ -583,7 +567,7 @@
         out_specs=vmem(),
         out_shape=jax.ShapeDtypeStruct((state_rows, node_total), jnp.bfloat16),
         scratch_shapes=total_scratch,
-        compiler_params=params(),
+        compiler_params=params(24),
         name="finish",
     )(faces, sides, previous, local, own, *halo)
     return closing(filtered, faces)

time: 272 us -> 252 us (0.926)
  Pallas kernels: 268 us -> 241 us
  local copies, waits for them, and re-layouts: 2.65 us -> 9.18 us
    pallas_call x3, Pallas kernels: 85.8 us -> 72.4 us  [body(): pl.pallas_call(functools.partial(next_kernel, k > 1), grid=(steps,), in_s...]
    unnamed x1 -> x19, local copies, waits for them, and re-layouts: 2.65 us -> 9.18 us
    pallas_call x2 -> x1, Pallas kernels: 47.3 us -> 41.1 us  [body(): pl.pallas_call(operators_kernel, grid=(cells // GROUP,), in_specs=[smem()...]
    pallas_call x1, Pallas kernels: 12.3 us -> 9.33 us  [body(): pl.pallas_call(last_kernel, in_specs=[smem()] * 2 + [vmem()] * 5, out_spe...]
where the time goes in v1:
time: 252 us; the launch traced here: 251 us
  Pallas kernels  241 us (96%)
  local copies, waits for them, and re-layouts  9.18 us (4%)
    pallas_call x1, Pallas kernels, closing(): pl.pallas_call(functools.partial(closing_kernel, domains, bands), in_spec...  96.1 us
    pallas_call x3, Pallas kernels, body(): pl.pallas_call(functools.partial(next_kernel, k > 1), grid=(steps,), in_s...  72.4 us
    pallas_call x1, Pallas kernels, body(): pl.pallas_call(operators_kernel, grid=(cells // GROUP,), in_specs=[smem()...  41.1 us
    pallas_call x4, Pallas kernels, exchange(): pl.pallas_call(functools.partial(exchange_kernel, lax.axis_size('dom')),...  22.5 us
    pallas_call x1, Pallas kernels, body(): pl.pallas_call(last_kernel, in_specs=[smem()] * 2 + [vmem()] * 5, out_spe...  9.33 us
    unnamed x19, local copies, waits for them, and re-layouts  9.18 us

profile of v1, /device:TPU:9, one launch (start us, length us, event | category | flops | bytes accessed | tf_op | source)
XLA Modules:
  0.0 251.4 jit_solution(2410459181716240042)
XLA Ops:
  0.0 0.0 copy-start.8
  0.0 0.0 copy-start.5
  0.7 0.1 add_convert_fusion.sides_ref
  0.8 41.1 %operators_and_first_apply.1 = (bf16[16,1024,512]{2,1,0:T(8,128)(2,1)}, f32[6144,128]{1,0:T(8,128)}, f32[6144,128]{1,0:T(8,128)}, bf16[512,128]{1,0:T(8,128)(2,1...) custom-call(s32[1]{0:T(128)S(6)} %copy.9.counts_ref, f32[32]{0:T(128)} %scale_ref.7, ...), custom_call_target="tpu_custom_call" | custom-call | tf_op jit(solution)/shard_map/operators_and_first_apply/pallas_call | solution.py:533
  41.8 0.0 copy-start.6
  41.8 0.9 copy-done.6
  42.7 0.0 copy-start.7
  42.7 0.9 copy-done.7
  43.6 5.0 %exchange.4 = (bf16[512,128]{1,0:T(8,128)(2,1)S(1)}, bf16[512,128]{1,0:T(8,128)(2,1)S(1)}) custom-call(bf16[512,128]{1,0:T(8,128)(2,1)S(1)} %copy-done.6, bf16[512,128]{1,0:T(8,128)(2,1)S(1)} %copy-done.7), custom_call_target="tpu_custom_call" | custom-call | tf_op jit(solution)/shard_map/exchange/pallas_call | solution.py:300
  48.6 0.0 copy-done.8
  48.6 0.0 copy-done.5
  48.6 0.0 copy-start
  48.6 1.9 copy-done
  50.5 0.0 copy-start.1
  50.5 1.4 copy-done.1
  51.9 0.0 copy-start.3
  51.9 1.9 copy-done.3
  53.8 0.0 copy-start.4
  53.8 1.0 copy-done.4
  54.9 0.0 copy-start.2
  54.9 23.6 %apply_next.3 = (f32[6144,128]{1,0:T(8,128)S(1)}, bf16[512,128]{1,0:T(8,128)(2,1)S(1)}, bf16[512,128]{1,0:T(8,128)(2,1)S(1)}, f32[1024,128]{1,0:T(8,128)S(1)}, bf16[6144,128]{1,0:T(8,128)(2,1)S(1)}) custom-call(s32[1]{0:T(128)S(6)} %copy.9.counts_ref, f32[32]{0:T(128)S(1)} %copy-done.8, s32[2,1024]{1,0:T(2,128)S(1)} %bitcast.4, ...), custom_call_target="tpu_custom_call" | custom-call | tf_op jit(solution)/shard_map/apply_next/pallas_call | solution.py:551
  78.4 7.2 %exchange.5 = (bf16[512,128]{1,0:T(8,128)(2,1)S(1)}, bf16[512,128]{1,0:T(8,128)(2,1)S(1)}) custom-call(bf16[512,128]{1,0:T(8,128)(2,1)S(1)} %get-tuple-element.45.left_ref, bf16[512,128]{1,0:T(8,128)(2,1)S(1)} %get-tuple-element.46.right_ref), custom_call_target="tpu_custom_call" | custom-call | tf_op jit(solution)/shard_map/exchange/pallas_call | solution.py:300
  85.7 0.0 copy-done.2
  85.7 23.8 %apply_next.4 = (f32[6144,128]{1,0:T(8,128)S(1)}, bf16[512,128]{1,0:T(8,128)(2,1)S(1)}, bf16[512,128]{1,0:T(8,128)(2,1)S(1)}, f32[1024,128]{1,0:T(8,128)S(1)}, bf16[6144,128]{1,0:T(8,128)(2,1)S(1)}) custom-call(s32[1]{0:T(128)S(6)} %copy.9.counts_ref, f32[32]{0:T(128)S(1)} %copy-done.8, s32[2,1024]{1,0:T(2,128)S(1)} %bitcast.5, ...), custom_call_target="tpu_custom_call" | custom-call | tf_op jit(solution)/shard_map/apply_next/pallas_call | solution.py:551
  109.5 5.3 %exchange.6 = (bf16[512,128]{1,0:T(8,128)(2,1)S(1)}, bf16[512,128]{1,0:T(8,128)(2,1)S(1)}) custom-call(bf16[512,128]{1,0:T(8,128)(2,1)S(1)} %get-tuple-element.53.left_ref, bf16[512,128]{1,0:T(8,128)(2,1)S(1)} %get-tuple-element.54.right_ref), custom_call_target="tpu_custom_call" | custom-call | tf_op jit(solution)/shard_map/exchange/pallas_call | solution.py:300
  114.8 25.0 %apply_next.5 = (f32[6144,128]{1,0:T(8,128)S(1)}, bf16[512,128]{1,0:T(8,128)(2,1)S(1)}, bf16[512,128]{1,0:T(8,128)(2,1)S(1)}, f32[1024,128]{1,0:T(8,128)S(1)}, bf16[6144,128]{1,0:T(8,128)(2,1)}) custom-call(s32[1]{0:T(128)S(6)} %copy.9.counts_ref, f32[32]{0:T(128)S(1)} %copy-done.8, s32[2,1024]{1,0:T(2,128)S(1)} %bitcast.6, s32[2]{0:T(128)S(1)} %add_convert_fusion.sides_ref, ...), custom_call_target="tpu_custom_call" | custom-call | tf_op jit(solution)/shard_map/apply_next/pallas_call | solution.py:551
  139.8 5.0 %exchange.7 = (bf16[512,128]{1,0:T(8,128)(2,1)S(1)}, bf16[512,128]{1,0:T(8,128)(2,1)S(1)}) custom-call(bf16[512,128]{1,0:T(8,128)(2,1)S(1)} %get-tuple-element.59.left_ref, bf16[512,128]{1,0:T(8,128)(2,1)S(1)} %get-tuple-element.60.right_ref), custom_call_target="tpu_custom_call" | custom-call | tf_op jit(solution)/shard_map/exchange/pallas_call | solution.py:300
  144.8 9.3 %finish.1.filtered_ref = bf16[64,12288]{1,0:T(8,128)(2,1)S(1)} custom-call(s32[2,1024]{1,0:T(2,128)S(1)} %bitcast.7, s32[2]{0:T(128)S(1)} %add_convert_fusion.sides_ref, bf16[6144,128]{1,0:T(8,128)(2,1)S(1)} %get-tuple-element.49.prev_ref, f32[6144,128]{1,0:T(8,128)S(1)} %get-tuple-element.57.old_ref, f32[1024,128]{1,0:T(8,128)S(1)} %get-tuple-element.58.old_own, ...), custom_call_target="tpu_custom_call" | custom-call | tf_op jit(solution)/shard_map/finish/pallas_call | solution.py:564
  154.1 96.1 %closing.1 = bf16[64,12288]{1,0:T(8,128)(2,1)S(1)} custom-call(bf16[64,12288]{1,0:T(8,128)(2,1)S(1)} %finish.1.filtered_ref, s32[2,1024]{1,0:T(2,128)S(1)} %bitcast.8), custom_call_target="tpu_custom_call" | custom-call | tf_op jit(solution)/shard_map/closing/pallas_call | solution.py:476
  250.3 1.1 copy.10
Async XLA Ops:
  0.0 48.6 %copy-start.8 = (f32[32]{0:T(128)S(1)}, f32[32]{0:T(128)}, u32[]{:S(2)}) copy-start(f32[32]{0:T(128)} %scale_ref.7) | copy-start | bytes 388
  0.0 48.6 %copy-start.5 = (s32[1,2,1024]{2,1,0:T(2,128)S(1)}, s32[1,2,1024]{2,1,0:T(2,128)}, u32[]{:S(2)}) copy-start(s32[1,2,1024]{2,1,0:T(2,128)} %param.12) | copy-start | bytes 24580
  41.8 0.9 copy-start.6
  42.7 0.9 copy-start.7
  48.6 1.9 copy-start
  50.5 1.4 copy-start.1
  51.9 1.9 copy-start.3
  53.8 1.0 copy-start.4
  54.9 30.8 %copy-start.2 = (bf16[6144,128]{1,0:T(8,128)(2,1)S(1)}, bf16[6144,128]{1,0:T(8,128)(2,1)}, u32[]{:S(2)}) copy-start(bf16[6144,128]{1,0:T(8,128)(2,1)} %get-tuple-element.36.prev_ref) | copy-start | bytes 4718596

commit v2 on v1

--- a/solution.py
+++ b/solution.py
@@ -542,7 +542,7 @@
             jax.ShapeDtypeStruct((half, lanes), jnp.float32),
         ] + outs,
         scratch_shapes=[pltpu.VMEM((node_total + tail, 1), jnp.float32)] + scratch,
-        compiler_params=params(),
+        compiler_params=params(32),
         name="operators_and_first_apply",
     )(cell_counts, cell_scale, faces, connectivity, cell_potential, cell_kinetic, states)
     current = previous
@@ -555,7 +555,7 @@
             out_specs=[vmem()] * 5,
             out_shape=outs,
             scratch_shapes=scratch,
-            compiler_params=params(32),
+            compiler_params=params(22),
             name="apply_next",
         )(cell_counts, cell_scale, faces, sides, ops, diag, previous, local, own, *halo)
         previous = current

time: 252 us -> 239 us (0.948)
  Pallas kernels: 241 us -> 226 us
  local copies, waits for them, and re-layouts: 9.18 us -> 12.4 us
    pallas_call x3, Pallas kernels: 72.4 us -> 60.2 us  [body(): pl.pallas_call(functools.partial(next_kernel, k > 1), grid=(steps,), in_s...]
    pallas_call x1, Pallas kernels: 41.1 us -> 37.4 us  [body(): pl.pallas_call(operators_kernel, grid=(cells // GROUP,), in_specs=[smem()...]
    unnamed x19, local copies, waits for them, and re-layouts: 9.18 us -> 12.4 us
where the time goes in v2:
time: 239 us
  Pallas kernels  226 us (95%)
  local copies, waits for them, and re-layouts  12.4 us (5%)
    pallas_call x1, Pallas kernels, closing(): pl.pallas_call(functools.partial(closing_kernel, domains, bands), in_spec...  96.1 us
    pallas_call x3, Pallas kernels, body(): pl.pallas_call(functools.partial(next_kernel, k > 1), grid=(steps,), in_s...  60.2 us
    pallas_call x1, Pallas kernels, body(): pl.pallas_call(operators_kernel, grid=(cells // GROUP,), in_specs=[smem()...  37.4 us
    pallas_call x4, Pallas kernels, exchange(): pl.pallas_call(functools.partial(exchange_kernel, lax.axis_size('dom')),...  22.5 us
    unnamed x19, local copies, waits for them, and re-layouts  12.4 us
    pallas_call x1, Pallas kernels, body(): pl.pallas_call(last_kernel, in_specs=[smem()] * 2 + [vmem()] * 5, out_spe...  9.33 us

profile of v2, /device:TPU:9, one launch (start us, length us, event | category | flops | bytes accessed | tf_op | source)
XLA Modules:
  0.0 238.8 jit_solution(694385332528770409)
XLA Ops:
  0.0 0.0 copy-start.8
  0.0 0.0 copy-start.4
  0.7 0.1 add_convert_fusion.sides_ref
  0.8 0.0 copy-start.1
  0.8 1.4 copy-done.1
  2.2 0.0 copy-start.2
  2.2 1.0 copy-done.2
  3.2 0.0 copy-start.3
  3.2 0.7 copy-done.3
  3.9 0.0 copy-start.5
  3.9 0.8 copy-done.5
  4.7 0.0 copy-start.6
  4.8 0.8 copy-done.6
  5.6 0.0 copy-start.7
  5.6 0.7 copy-done.7
  6.2 37.4 %operators_and_first_apply.1 = (bf16[16,1024,512]{2,1,0:T(8,128)(2,1)}, f32[6144,128]{1,0:T(8,128)S(1)}, f32[6144,128]{1,0:T(8,128)S(1)}, bf16[512,128]{1,0:T(8,...) custom-call(s32[1]{0:T(128)S(6)} %copy.9.counts_ref, ...), custom_call_target="tpu_custom_call" | custom-call | tf_op jit(solution)/shard_map/operators_and_first_apply/pallas_call | solution.py:533
  43.6 5.0 %exchange.4 = (bf16[512,128]{1,0:T(8,128)(2,1)S(1)}, bf16[512,128]{1,0:T(8,128)(2,1)S(1)}) custom-call(bf16[512,128]{1,0:T(8,128)(2,1)S(1)} %get-tuple-element.39.left_ref, bf16[512,128]{1,0:T(8,128)(2,1)S(1)} %get-tuple-element.40.right_ref), custom_call_target="tpu_custom_call" | custom-call | tf_op jit(solution)/shard_map/exchange/pallas_call | solution.py:300
  48.6 0.0 copy-done.8
  48.6 0.0 copy-done.4
  48.6 0.0 copy-start
  48.6 5.8 %copy-done = bf16[16,1024,512]{2,1,0:T(8,128)(2,1)S(1)} copy-done((bf16[16,1024,512]{2,1,0:T(8,128)(2,1)S(1)}, bf16[16,1024,512]{2,1,0:T(8,128)(2,1)}, u32[]{:S(2)}) %copy-start) | copy-done | bytes 16777240
  54.4 19.4 %apply_next.3 = (f32[6144,128]{1,0:T(8,128)S(1)}, bf16[512,128]{1,0:T(8,128)(2,1)S(1)}, bf16[512,128]{1,0:T(8,128)(2,1)S(1)}, f32[1024,128]{1,0:T(8,128)S(1)}, bf16[6144,128]{1,0:T(8,128)(2,1)S(1)}) custom-call(s32[1]{0:T(128)S(6)} %copy.9.counts_ref, f32[32]{0:T(128)S(1)} %copy-done.8, s32[2,1024]{1,0:T(2,128)S(1)} %bitcast.4, ...), custom_call_target="tpu_custom_call" | custom-call | tf_op jit(solution)/shard_map/apply_next/pallas_call | solution.py:551
  73.8 7.2 %exchange.5 = (bf16[512,128]{1,0:T(8,128)(2,1)S(1)}, bf16[512,128]{1,0:T(8,128)(2,1)S(1)}) custom-call(bf16[512,128]{1,0:T(8,128)(2,1)S(1)} %get-tuple-element.45.left_ref, bf16[512,128]{1,0:T(8,128)(2,1)S(1)} %get-tuple-element.46.right_ref), custom_call_target="tpu_custom_call" | custom-call | tf_op jit(solution)/shard_map/exchange/pallas_call | solution.py:300
  81.1 19.8 %apply_next.4 = (f32[6144,128]{1,0:T(8,128)S(1)}, bf16[512,128]{1,0:T(8,128)(2,1)S(1)}, bf16[512,128]{1,0:T(8,128)(2,1)S(1)}, f32[1024,128]{1,0:T(8,128)S(1)}, bf16[6144,128]{1,0:T(8,128)(2,1)S(1)}) custom-call(s32[1]{0:T(128)S(6)} %copy.9.counts_ref, f32[32]{0:T(128)S(1)} %copy-done.8, s32[2,1024]{1,0:T(2,128)S(1)} %bitcast.5, ...), custom_call_target="tpu_custom_call" | custom-call | tf_op jit(solution)/shard_map/apply_next/pallas_call | solution.py:551
  100.9 5.3 %exchange.6 = (bf16[512,128]{1,0:T(8,128)(2,1)S(1)}, bf16[512,128]{1,0:T(8,128)(2,1)S(1)}) custom-call(bf16[512,128]{1,0:T(8,128)(2,1)S(1)} %get-tuple-element.53.left_ref, bf16[512,128]{1,0:T(8,128)(2,1)S(1)} %get-tuple-element.54.right_ref), custom_call_target="tpu_custom_call" | custom-call | tf_op jit(solution)/shard_map/exchange/pallas_call | solution.py:300
  106.2 21.0 %apply_next.5 = (f32[6144,128]{1,0:T(8,128)S(1)}, bf16[512,128]{1,0:T(8,128)(2,1)S(1)}, bf16[512,128]{1,0:T(8,128)(2,1)S(1)}, f32[1024,128]{1,0:T(8,128)S(1)}, bf16[6144,128]{1,0:T(8,128)(2,1)}) custom-call(s32[1]{0:T(128)S(6)} %copy.9.counts_ref, f32[32]{0:T(128)S(1)} %copy-done.8, s32[2,1024]{1,0:T(2,128)S(1)} %bitcast.6, s32[2]{0:T(128)S(1)} %add_convert_fusion.sides_ref, ...), custom_call_target="tpu_custom_call" | custom-call | tf_op jit(solution)/shard_map/apply_next/pallas_call | solution.py:551
  127.2 5.0 %exchange.7 = (bf16[512,128]{1,0:T(8,128)(2,1)S(1)}, bf16[512,128]{1,0:T(8,128)(2,1)S(1)}) custom-call(bf16[512,128]{1,0:T(8,128)(2,1)S(1)} %get-tuple-element.59.left_ref, bf16[512,128]{1,0:T(8,128)(2,1)S(1)} %get-tuple-element.60.right_ref), custom_call_target="tpu_custom_call" | custom-call | tf_op jit(solution)/shard_map/exchange/pallas_call | solution.py:300
  132.2 9.3 %finish.1.filtered_ref = bf16[64,12288]{1,0:T(8,128)(2,1)S(1)} custom-call(s32[2,1024]{1,0:T(2,128)S(1)} %bitcast.7, s32[2]{0:T(128)S(1)} %add_convert_fusion.sides_ref, bf16[6144,128]{1,0:T(8,128)(2,1)S(1)} %get-tuple-element.49.prev_ref, f32[6144,128]{1,0:T(8,128)S(1)} %get-tuple-element.57.old_ref, f32[1024,128]{1,0:T(8,128)S(1)} %get-tuple-element.58.old_own, ...), custom_call_target="tpu_custom_call" | custom-call | tf_op jit(solution)/shard_map/finish/pallas_call | solution.py:564
  141.5 96.1 %closing.1 = bf16[64,12288]{1,0:T(8,128)(2,1)S(1)} custom-call(bf16[64,12288]{1,0:T(8,128)(2,1)S(1)} %finish.1.filtered_ref, s32[2,1024]{1,0:T(2,128)S(1)} %bitcast.8), custom_call_target="tpu_custom_call" | custom-call | tf_op jit(solution)/shard_map/closing/pallas_call | solution.py:476
  237.6 1.1 copy.10
Async XLA Ops:
  0.0 48.6 %copy-start.8 = (f32[32]{0:T(128)S(1)}, f32[32]{0:T(128)}, u32[]{:S(2)}) copy-start(f32[32]{0:T(128)} %scale_ref.7) | copy-start | bytes 388
  0.0 48.6 %copy-start.4 = (s32[1,2,1024]{2,1,0:T(2,128)S(1)}, s32[1,2,1024]{2,1,0:T(2,128)}, u32[]{:S(2)}) copy-start(s32[1,2,1024]{2,1,0:T(2,128)} %param.12) | copy-start | bytes 24580
  0.8 1.4 copy-start.1
  2.2 1.0 copy-start.2
  3.2 0.7 copy-start.3
  3.9 0.8 copy-start.5
  4.7 0.8 copy-start.6
  5.6 0.7 copy-start.7
  48.6 5.8 %copy-start = (bf16[16,1024,512]{2,1,0:T(8,128)(2,1)S(1)}, bf16[16,1024,512]{2,1,0:T(8,128)(2,1)}, u32[]{:S(2)}) copy-start(bf16[16,1024,512]{2,1,0:T(8,128)(2,1)} %get-tuple-element.34.ops_ref) | copy-start | bytes 50331652

commit v3 on v2

--- a/solution.py
+++ b/solution.py
@@ -526,8 +526,8 @@
         pltpu.VMEM((half + tail, lanes), jnp.bfloat16),
         pltpu.VMEM((half + tail, lanes), jnp.float32),
     ] + total_scratch
-    group = GROUP // 2
-    steps = cells // GROUP
+    group = GROUP
+    steps = cells // (2 * GROUP)
     ops_spec = pl.BlockSpec((group, 2 * width, width), lambda g: (g, 0, 0))
     blocks = cells // 2 // GROUP
     ops, diag, local, left, right, own, previous = pl.pallas_call(
@@ -555,7 +555,7 @@
             out_specs=[vmem()] * 5,
             out_shape=outs,
             scratch_shapes=scratch,
-            compiler_params=params(22),
+            compiler_params=params(27),
             name="apply_next",
         )(cell_counts, cell_scale, faces, sides, ops, diag, previous, local, own, *halo)
         previous = current

time: 239 us -> 239 us (level)
  local copies, waits for them, and re-layouts: 12.4 us -> 6.64 us
  Pallas kernels: 226 us -> 231 us
    pallas_call x3, Pallas kernels: 60.2 us -> 66.1 us  [body(): pl.pallas_call(functools.partial(next_kernel, k > 1), grid=(steps,), in_s...]
    unnamed x19 -> x17, local copies, waits for them, and re-layouts: 12.4 us -> 6.64 us
where the time goes in v3:
time: 239 us
  Pallas kernels  231 us (97%)
  local copies, waits for them, and re-layouts  6.64 us (3%)
    pallas_call x1, Pallas kernels, closing(): pl.pallas_call(functools.partial(closing_kernel, domains, bands), in_spec...  96.2 us
    pallas_call x3, Pallas kernels, body(): pl.pallas_call(functools.partial(next_kernel, k > 1), grid=(steps,), in_s...  66.1 us
    pallas_call x1, Pallas kernels, body(): pl.pallas_call(operators_kernel, grid=(cells // GROUP,), in_specs=[smem()...  37.4 us
    pallas_call x4, Pallas kernels, exchange(): pl.pallas_call(functools.partial(exchange_kernel, lax.axis_size('dom')),...  22.5 us
    pallas_call x1, Pallas kernels, body(): pl.pallas_call(last_kernel, in_specs=[smem()] * 2 + [vmem()] * 5, out_spe...  9.33 us
    unnamed x17, local copies, waits for them, and re-layouts  6.64 us

profile of v3, /device:TPU:9, one launch (start us, length us, event | category | flops | bytes accessed | tf_op | source)
XLA Modules:
  0.0 238.9 jit_solution(371948243806126619)
XLA Ops:
  0.7 0.1 add_convert_fusion.sides_ref
  0.7 0.0 copy-start
  0.7 1.4 copy-done
  2.1 0.0 copy-start.1
  2.1 1.0 copy-done.1
  3.2 0.0 copy-start.2
  3.2 0.7 copy-done.2
  3.9 0.0 copy-start.4
  3.9 0.8 copy-done.4
  4.7 0.0 copy-start.5
  4.7 0.8 copy-done.5
  5.6 0.0 copy-start.6
  5.6 0.7 copy-done.6
  6.2 37.4 %operators_and_first_apply.1 = (bf16[16,1024,512]{2,1,0:T(8,128)(2,1)}, f32[6144,128]{1,0:T(8,128)S(1)}, f32[6144,128]{1,0:T(8,128)S(1)}, bf16[512,128]{1,0:T(8,...) custom-call(s32[1]{0:T(128)S(6)} %copy.9.counts_ref, ...), custom_call_target="tpu_custom_call" | custom-call | tf_op jit(solution)/shard_map/operators_and_first_apply/pallas_call | solution.py:533
  43.6 5.0 %exchange.4 = (bf16[512,128]{1,0:T(8,128)(2,1)S(1)}, bf16[512,128]{1,0:T(8,128)(2,1)S(1)}) custom-call(bf16[512,128]{1,0:T(8,128)(2,1)S(1)} %get-tuple-element.39.left_ref, bf16[512,128]{1,0:T(8,128)(2,1)S(1)} %get-tuple-element.40.right_ref), custom_call_target="tpu_custom_call" | custom-call | tf_op jit(solution)/shard_map/exchange/pallas_call | solution.py:300
  48.6 0.0 copy-start.3
  48.6 0.0 copy-start.7
  48.6 21.4 %apply_next.3 = (f32[6144,128]{1,0:T(8,128)S(1)}, bf16[512,128]{1,0:T(8,128)(2,1)S(1)}, bf16[512,128]{1,0:T(8,128)(2,1)S(1)}, f32[1024,128]{1,0:T(8,128)S(1)}, bf16[6144,128]{1,0:T(8,128)(2,1)S(1)}) custom-call(s32[1]{0:T(128)S(6)} %copy.9.counts_ref, f32[32]{0:T(128)S(1)} %copy-done.6, s32[2,1024]{1,0:T(2,128)S(1)} %bitcast.4, ...), custom_call_target="tpu_custom_call" | custom-call | tf_op jit(solution)/shard_map/apply_next/pallas_call | solution.py:551
  70.0 7.2 %exchange.5 = (bf16[512,128]{1,0:T(8,128)(2,1)S(1)}, bf16[512,128]{1,0:T(8,128)(2,1)S(1)}) custom-call(bf16[512,128]{1,0:T(8,128)(2,1)S(1)} %get-tuple-element.45.left_ref, bf16[512,128]{1,0:T(8,128)(2,1)S(1)} %get-tuple-element.46.right_ref), custom_call_target="tpu_custom_call" | custom-call | tf_op jit(solution)/shard_map/exchange/pallas_call | solution.py:300
  77.2 0.0 copy-done.3
  77.2 0.0 copy-done.7
  77.3 21.8 %apply_next.4 = (f32[6144,128]{1,0:T(8,128)S(1)}, bf16[512,128]{1,0:T(8,128)(2,1)S(1)}, bf16[512,128]{1,0:T(8,128)(2,1)S(1)}, f32[1024,128]{1,0:T(8,128)S(1)}, bf16[6144,128]{1,0:T(8,128)(2,1)S(1)}) custom-call(s32[1]{0:T(128)S(6)} %copy.9.counts_ref, f32[32]{0:T(128)S(1)} %copy-done.7, s32[2,1024]{1,0:T(2,128)S(1)} %bitcast.5, ...), custom_call_target="tpu_custom_call" | custom-call | tf_op jit(solution)/shard_map/apply_next/pallas_call | solution.py:551
  99.0 5.3 %exchange.6 = (bf16[512,128]{1,0:T(8,128)(2,1)S(1)}, bf16[512,128]{1,0:T(8,128)(2,1)S(1)}) custom-call(bf16[512,128]{1,0:T(8,128)(2,1)S(1)} %get-tuple-element.53.left_ref, bf16[512,128]{1,0:T(8,128)(2,1)S(1)} %get-tuple-element.54.right_ref), custom_call_target="tpu_custom_call" | custom-call | tf_op jit(solution)/shard_map/exchange/pallas_call | solution.py:300
  104.3 22.9 %apply_next.5 = (f32[6144,128]{1,0:T(8,128)S(1)}, bf16[512,128]{1,0:T(8,128)(2,1)S(1)}, bf16[512,128]{1,0:T(8,128)(2,1)S(1)}, f32[1024,128]{1,0:T(8,128)S(1)}, bf16[6144,128]{1,0:T(8,128)(2,1)}) custom-call(s32[1]{0:T(128)S(6)} %copy.9.counts_ref, f32[32]{0:T(128)S(1)} %copy-done.7, s32[2,1024]{1,0:T(2,128)S(1)} %bitcast.6, s32[2]{0:T(128)S(1)} %add_convert_fusion.sides_ref, ...), custom_call_target="tpu_custom_call" | custom-call | tf_op jit(solution)/shard_map/apply_next/pallas_call | solution.py:551
  127.2 5.0 %exchange.7 = (bf16[512,128]{1,0:T(8,128)(2,1)S(1)}, bf16[512,128]{1,0:T(8,128)(2,1)S(1)}) custom-call(bf16[512,128]{1,0:T(8,128)(2,1)S(1)} %get-tuple-element.59.left_ref, bf16[512,128]{1,0:T(8,128)(2,1)S(1)} %get-tuple-element.60.right_ref), custom_call_target="tpu_custom_call" | custom-call | tf_op jit(solution)/shard_map/exchange/pallas_call | solution.py:300
  132.2 9.3 %finish.1.filtered_ref = bf16[64,12288]{1,0:T(8,128)(2,1)S(1)} custom-call(s32[2,1024]{1,0:T(2,128)S(1)} %bitcast.7, s32[2]{0:T(128)S(1)} %add_convert_fusion.sides_ref, bf16[6144,128]{1,0:T(8,128)(2,1)S(1)} %get-tuple-element.49.prev_ref, f32[6144,128]{1,0:T(8,128)S(1)} %get-tuple-element.57.old_ref, f32[1024,128]{1,0:T(8,128)S(1)} %get-tuple-element.58.old_own, ...), custom_call_target="tpu_custom_call" | custom-call | tf_op jit(solution)/shard_map/finish/pallas_call | solution.py:564
  141.6 96.2 %closing.1 = bf16[64,12288]{1,0:T(8,128)(2,1)S(1)} custom-call(bf16[64,12288]{1,0:T(8,128)(2,1)S(1)} %finish.1.filtered_ref, s32[2,1024]{1,0:T(2,128)S(1)} %bitcast.8), custom_call_target="tpu_custom_call" | custom-call | tf_op jit(solution)/shard_map/closing/pallas_call | solution.py:476
  237.8 1.1 copy.10
Async XLA Ops:
  0.7 1.4 copy-start
  2.1 1.0 copy-start.1
  3.2 0.7 copy-start.2
  3.9 0.8 copy-start.4
  4.7 0.8 copy-start.5
  5.6 0.7 copy-start.6
  48.6 28.7 %copy-start.3 = (s32[1,2,1024]{2,1,0:T(2,128)S(1)}, s32[1,2,1024]{2,1,0:T(2,128)}, u32[]{:S(2)}) copy-start(s32[1,2,1024]{2,1,0:T(2,128)} %param.12) | copy-start | bytes 24580
  48.6 28.7 %copy-start.7 = (f32[32]{0:T(128)S(1)}, f32[32]{0:T(128)}, u32[]{:S(2)}) copy-start(f32[32]{0:T(128)} %scale_ref.7) | copy-start | bytes 388
